TPU v7x, 128 devices: a whole 4x4x4 slice. The times are simulated.
128 devices in a mesh: ctx: 32 (over z, y_hi, x), wa: 4 (over y_lo, core).
Axes of the slice: x: 4, y: 4 (y_hi: 2, y_lo: 2; y = y_hi * 2 + y_lo), z: 4, core: 2. Of those that a mesh axis runs over, the one named last changes fastest.
Arguments:
- tokens: bfloat16 [4096, 8192], P('ctx', 'wa')
- norm_gain: bfloat16 [8192], P('wa'), may hold values from 0.5 to 1.5
- w_query: bfloat16 [8192, 4096], P('wa'), may hold values from -0.0625 to 0.0625
- keyvalue_weight: bfloat16 [8192, 1024], P('wa'), may hold values from -0.0625 to 0.0625
- cache_keyval: bfloat16 [65536, 1024], P('ctx', 'wa')
- kept_blocks: int32 [32, 3], P('ctx'), may hold values from 0 to 15, as said below
- kept_counts: int32 [32], P('ctx'), may hold values from 1 to 3, as said below
Outputs:
- attended: bfloat16 [4096, 4096], P('ctx', 'wa')
Inputs may be any that keep to these rules, and one draw needn't show every extreme that they name: `kept_blocks`: within one row the indices are distinct. `kept_counts`: some shard uses exactly 3 slots.
All inputs are finite; a program needn't handle non-finite values.
Results may differ from a plain program's by a relative error of at most 0.0095.
The roundings to bfloat16 on the way count: a program that leaves them out, or rounds other values in their place, can miss the bound.
Values may be sent and summed in bfloat16 or wider, within the bound.
No kernel may reach another device: no remote copies, remote signals or barrier semaphores. Data moves between devices by JAX's collectives and lax.ppermute only.
A program may use at most 192 MiB of HBM per device.

v0:
```python
import math
import jax
import jax.numpy as jnp
from jax import lax
from jax.sharding import PartitionSpec as P

HEAD_WIDTH = 128
BLOCK = 128
MAXB = 3


def attend(carry, kv_rows, visible, queries_four):
    top, total, summed = carry
    heads_local = queries_four.shape[1]
    rows_block = kv_rows.reshape(kv_rows.shape[0], heads_local, 2, HEAD_WIDTH)
    keys_part = rows_block[:, :, 0, :]
    values_part = rows_block[:, :, 1, :]
    scores = jnp.einsum(
        "thgd,khd->htgk", queries_four, keys_part, preferred_element_type=jnp.float32
    )
    mask_full = visible[None, :, None, :]
    masked = jnp.where(mask_full, scores, -1e30)
    new_top = jnp.maximum(top, jnp.max(masked, axis=-1))
    weights = jnp.where(mask_full, jnp.exp(masked - new_top[..., None]), 0.0)
    factor = jnp.exp(top - new_top)
    total = total * factor + jnp.sum(weights, axis=-1)
    mixed = jnp.einsum(
        "htgk,khd->htgd",
        weights.astype(jnp.bfloat16),
        values_part,
        preferred_element_type=jnp.float32,
    )
    summed = summed * factor[..., None] + mixed
    return (new_top, total, summed)


def fold_rows(carry, kv_rows, mask_maker, queries_four):
    count_rows = kv_rows.shape[0]
    width_block = math.gcd(count_rows, 512)

    def advance(position, state):
        offset = position * width_block
        rows_now = lax.dynamic_slice_in_dim(kv_rows, offset, width_block, 0)
        visible = mask_maker(offset, offset, width_block)
        return attend(state, rows_now, visible, queries_four)

    return lax.fori_loop(0, count_rows // width_block, advance, carry)


def on_device(tokens, norm_gain, w_query, keyvalue_weight, cache_keyval, kept_blocks, kept_counts):
    tok_rows = tokens.shape[0]
    whole, gain_whole = (
        lax.all_gather(tokens, "wa", axis=1, tiled=True),
        lax.all_gather(norm_gain, "wa", axis=0, tiled=True),
    )
    values = whole.astype(jnp.float32)
    meansq = jnp.mean(values * values, axis=1, keepdims=True)
    normed = (values * lax.rsqrt(meansq + 1e-05) * gain_whole.astype(jnp.float32)[None, :]).astype(
        jnp.bfloat16
    )
    query_cols, keyval_cols = (
        lax.all_to_all(w_query, "wa", split_axis=1, concat_axis=0, tiled=True),
        lax.all_to_all(keyvalue_weight, "wa", split_axis=1, concat_axis=0, tiled=True),
    )
    query_sum = jnp.dot(normed, query_cols, preferred_element_type=jnp.float32)
    keyval_sum = jnp.dot(normed, keyval_cols, preferred_element_type=jnp.float32)
    queries = (query_sum * HEAD_WIDTH ** (-0.5)).astype(jnp.bfloat16)
    new_keyval = keyval_sum.astype(jnp.bfloat16)
    heads_local = new_keyval.shape[1] // (2 * HEAD_WIDTH)
    head_group = queries.shape[1] // (heads_local * HEAD_WIDTH)
    queries_four = queries.reshape(tok_rows, heads_local, head_group, HEAD_WIDTH)
    width_local = cache_keyval.shape[1]
    block_count = cache_keyval.shape[0] // BLOCK
    picked = cache_keyval.reshape(block_count, BLOCK, width_local)[kept_blocks[0]]
    kept_rows = picked.reshape(MAXB * BLOCK, width_local)
    slot_ids = jnp.arange(MAXB * BLOCK) // BLOCK
    live_flags = (slot_ids < kept_counts[0]).astype(jnp.bfloat16)
    my_shard = lax.axis_index("ctx")
    query_index = my_shard * tok_rows + jnp.arange(tok_rows)
    init = (
        jnp.full((heads_local, tok_rows, head_group), -1e30, jnp.float32),
        jnp.zeros((heads_local, tok_rows, head_group), jnp.float32),
        jnp.zeros((heads_local, tok_rows, head_group, HEAD_WIDTH), jnp.float32),
    )
    rows_piece = lax.all_gather(kept_rows, "ctx", axis=0, tiled=True)
    live_piece = lax.all_gather(live_flags, "ctx", axis=0, tiled=True)

    def cache_mask(global_start, offset, width_block):
        live_now = lax.dynamic_slice_in_dim(live_piece, offset, width_block, 0) > 0
        return jnp.broadcast_to(live_now[None, :], (tok_rows, width_block))

    carried = fold_rows(init, rows_piece, cache_mask, queries_four)

    def span_mask(global_start, offset, width_block):
        key_index = global_start + jnp.arange(width_block)
        return key_index[None, :] <= query_index[:, None]

    carried = fold_rows(
        carried, lax.all_gather(new_keyval, "ctx", axis=0, tiled=True), span_mask, queries_four
    )
    final_top, final_total, final_sum = carried
    result = final_sum / final_total[..., None]
    result = jnp.transpose(result, (1, 0, 2, 3)).reshape(
        tok_rows, heads_local * head_group * HEAD_WIDTH
    )
    return result.astype(jnp.bfloat16)


def solution(mesh):
    return jax.shard_map(
        on_device,
        mesh=mesh,
        in_specs=(
            P("ctx", "wa"),
            P("wa"),
            P("wa", None),
            P("wa", None),
            P("ctx", "wa"),
            P("ctx", None),
            P("ctx"),
        ),
        out_specs=P("ctx", "wa"),
        check_vma=False,
    )
```

profile of v0, /device:TPU:0, one launch (start us, length us, event | category | flops | bytes accessed | tf_op | source)
XLA Modules:
  0.0 598.3 jit_solution(6876186711223215149)
XLA Ops:
  6.5 6.6 %copy.48 = bf16[2048,1024]{0,1:T(8,128)(2,1)} copy(bf16[2048,1024]{1,0:T(8,128)(2,1)} %param.14) | data formatting | bytes 8388608 | tf_op args[3]
  13.1 4.9 all-to-all-start.1
  18.7 22.6 %copy.44 = bf16[2048,4096]{0,1:T(8,128)(2,1)} copy(bf16[2048,4096]{1,0:T(8,128)(2,1)} %param.13) | data formatting | bytes 33554432 | tf_op args[2]
  41.3 41.8 %all-to-all-done.1 = bf16[2048,4,256]{0,2,1:T(8,128)(2,1)} async-done(((bf16[2048,4,256]{0,2,1:T(8,128)(2,1)}), bf16[2048,4,256]{0,2,1:T(8,128)(2,1)}, u32[]{:S(2)}, u32[]{:S(2)}) %all-to-all-start.1) | async-done | bytes 4194336 | tf_op jit(solution)/shard_map/all_to_all | solution.py:63
  83.1 7.1 %all-to-all-start = ((bf16[2048,4,1024]{0,2,1:T(8,128)(2,1)}), bf16[2048,4,1024]{0,2,1:T(8,128)(2,1)}, u32[]{:S(2)}, u32[]{:S(2)}) async-start(bf16[2048,4,1024]{0,2,1:T(8,128)(2,1)} %bitcast.159), calls=%async_computation | async-start | bytes 33554432 | tf_op jit(solution)/shard_map/all_to_all | solution.py:62
  90.3 1.2 gather_fusion
  91.6 212.0 %all_gather.18 = bf16[8192]{0:T(1024)(128)(2,1)S(1)} all-gather(bf16[2048]{0:T(1024)(128)(2,1)S(1)} %copy-done.5), channel_id=1, replica_groups=mesh['ctx'=32,'wa'=4] {'wa'}, dimensions={0}, use_global_device_ids=true | all-gather | bytes 20480 | tf_op jit(solution)/shard_map/all_gather | solution.py:54
  304.3 96.4 %all-gather = bf16[32,1,384]{2,1,0:T(2,128)(2,1)S(1)} all-gather(bf16[1,1,384]{2,1,0:T(2,128)(2,1)S(1)} %reshape.207), channel_id=1, replica_groups=mesh['ctx'=32,'wa'=4] {'ctx'}, dimensions={0}, use_global_device_ids=true | all-gather | bytes 25344 | tf_op jit(solution)/shard_map/all_gather | solution.py:86
  400.9 6.2 %copy.49 = bf16[4,2048,256]{2,1,0:T(8,128)(2,1)} copy(bf16[4,2048,256]{1,2,0:T(8,128)(2,1)} %bitcast.9) | data formatting | bytes 8388608 | tf_op jit(solution)/shard_map/all_to_all | solution.py:63
  407.2 2.2 fusion.32
  409.4 3.6 convolution_convert_fusion
  413.0 22.6 %copy.45 = bf16[4,2048,1024]{2,1,0:T(8,128)(2,1)} copy(bf16[4,2048,1024]{1,2,0:T(8,128)(2,1)} %bitcast.6) | data formatting | bytes 33554432 | tf_op jit(solution)/shard_map/all_to_all | solution.py:62
  435.6 8.2 %fusion.36 = bf16[16,8,8,128]{3,1,2,0:T(8,128)(2,1)S(1)} fusion(bf16[8192,1024]{1,0:T(8,128)(2,1)} %bitcast.160, bf16[128,8192]{1,0:T(8,128)(2,1)S(1)} %copy-done.2, f32[8192]{0:T(1024)S(1)} %convert_element_type.42, f32[128]{0:T(128)S(1)} %add_rsqrt_fusion), kind=kOutput, calls=%fused_computation.61 | convolution fusion | flops 2151940096 | bytes 19169792 | tf_op jit(solution)/shard_map/dot_general | solution.py:65
  444.0 117.9 %while.37 = (s32[]{:T(128)}, f32[1,128,8]{1,2,0:T(8,128)S(1)}, f32[1,128,8]{1,2,0:T(8,128)S(1)}, f32[1,128,8,128]{3,1,2,0:T(8,128)}, bf16[12288]{0:T(1024)(128)(...) while((s32[]{:T(128)}, f32[1,128,8]{1,2,0:T(8,128)S(1)}, ...), condition=%wide.region_4.5_spmd.clone, body=%wide.region_1.4_spmd.clone.sunk | while | flops 274079232 | bytes 8982191 | solution.py:47
  444.1 1.0 constant_dynamic-slice_fusion.5
  445.7 1.6 fusion.64
  448.0 1.0 constant_dynamic-slice_fusion.5
  449.7 2.7 fusion.64
  453.0 1.0 constant_dynamic-slice_fusion.5
  454.6 2.7 fusion.64
  457.9 1.0 constant_dynamic-slice_fusion.5
  459.6 2.7 fusion.64
  462.9 1.0 constant_dynamic-slice_fusion.5
  464.5 2.7 fusion.64
  467.9 1.0 constant_dynamic-slice_fusion.5
  469.5 2.7 fusion.64
  472.8 1.0 constant_dynamic-slice_fusion.5
  474.4 2.7 fusion.64
  477.8 1.0 constant_dynamic-slice_fusion.5
  479.4 2.7 fusion.64
  482.7 1.0 constant_dynamic-slice_fusion.5
  484.3 2.7 fusion.64
  487.7 1.0 constant_dynamic-slice_fusion.5
  489.3 2.7 fusion.64
  492.6 1.0 constant_dynamic-slice_fusion.5
  494.3 2.7 fusion.64
  497.6 1.0 constant_dynamic-slice_fusion.5
  499.2 2.7 fusion.64
  504.2 2.7 fusion.64
  509.1 2.7 fusion.64
  514.1 2.7 fusion.64
  519.0 2.7 fusion.64
  524.0 2.7 fusion.64
  527.3 1.0 constant_dynamic-slice_fusion.5
  528.9 2.7 fusion.64
  533.9 2.7 fusion.64
  537.2 1.0 constant_dynamic-slice_fusion.5
  538.9 2.7 fusion.64
  543.8 2.7 fusion.64
  547.2 1.0 constant_dynamic-slice_fusion.5
  548.8 2.7 fusion.64
  553.7 2.7 fusion.64
  557.1 1.0 constant_dynamic-slice_fusion.5
  558.7 2.7 fusion.64
  562.0 27.5 %while.36 = (s32[]{:T(128)}, f32[1,128,8]{1,2,0:T(8,128)S(1)}, f32[1,128,8]{1,2,0:T(8,128)S(1)}, f32[1,128,8,128]{3,1,2,0:T(8,128)}, bf16[4096,256]{1,0:T(8,128)...) while((s32[]{:T(128)}, f32[1,128,8]{1,2,0:T(8,128)S(1)}, ...), condition=%wide.region_8.9_spmd.clone, body=%wide.region_5.8_spmd.clone.sunk | while | flops 274009728 | bytes 13440223 | solution.py:47
  562.0 1.0 constant_dynamic-slice_fusion.4
  565.4 1.0 constant_dynamic-slice_fusion.4
  568.9 1.0 constant_dynamic-slice_fusion.4
  572.3 1.0 constant_dynamic-slice_fusion.4
  575.7 1.0 constant_dynamic-slice_fusion.4
  579.2 1.0 constant_dynamic-slice_fusion.4
  582.6 1.0 constant_dynamic-slice_fusion.4
  586.0 1.0 constant_dynamic-slice_fusion.4
  589.5 1.3 divide_convert_fusion
  (323 shorter events, 58.4 us)
Async XLA Ops:
  6.5 83.7 %copy-start = (bf16[2048,256]{1,0:T(8,128)(2,1)S(1)}, bf16[2048,256]{1,0:T(8,128)(2,1)}, u32[]{:S(2)}) copy-start(bf16[2048,256]{1,0:T(8,128)(2,1)} %param.15) | copy-start | bytes 3145732
  13.1 70.0 %all-to-all-start.1 = ((bf16[2048,4,256]{0,2,1:T(8,128)(2,1)}), bf16[2048,4,256]{0,2,1:T(8,128)(2,1)}, u32[]{:S(2)}, u32[]{:S(2)}) async-start(bf16[2048,4,256]{0,2,1:T(8,128)(2,1)} %bitcast.161), calls=%async_computation.1 | async-start | bytes 8388608 | tf_op jit(solution)/shard_map/all_to_all | solution.py:63
  18.0 389.2 %all-gather.7.cloned.1.call-start = ((), (), s32[]{:S(2)}) async-start(), calls=%async_computation.3 | async-start | bytes 2621440 | tf_op jit(solution)/shard_map/all_gather | solution.py:53
  83.1 7.2 %copy-start.6 = (s32[1,3]{1,0:T(1,128)S(1)}, s32[1,3]{1,0:T(1,128)}, u32[]{:S(2)}) copy-start(s32[1,3]{1,0:T(1,128)} %param.16) | copy-start | bytes 40
  83.1 8.6 %copy-start.5 = (bf16[2048]{0:T(1024)(128)(2,1)S(1)}, bf16[2048]{0:T(1024)(128)(2,1)}, u32[]{:S(2)}) copy-start(bf16[2048]{0:T(1024)(128)(2,1)} %param.12) | copy-start | bytes 12292
  83.1 329.9 %all-to-all-start = ((bf16[2048,4,1024]{0,2,1:T(8,128)(2,1)}), bf16[2048,4,1024]{0,2,1:T(8,128)(2,1)}, u32[]{:S(2)}, u32[]{:S(2)}) async-start(bf16[2048,4,1024]{0,2,1:T(8,128)(2,1)} %bitcast.159), calls=%async_computation | async-start | bytes 33554432 | tf_op jit(solution)/shard_map/all_to_all | solution.py:62
  90.2 353.8 %all-gather.5.cloned.1.call-start = ((), (), s32[]{:S(2)}) async-start(), calls=%async_computation.2 | async-start | bytes 6488064 | tf_op jit(solution)/shard_map/all_gather | solution.py:85
  91.5 470.4 %all-gather.9.cloned.1.call-start = ((), (), s32[]{:S(2)}) async-start(), calls=%async_computation.4 | async-start | bytes 2162688 | tf_op jit(solution)/shard_map/all_gather | solution.py:99
  407.2 2.2 copy-start.2
  562.0 1.9 copy-start.3
  564.6 0.8 copy-start.4
  565.4 1.8 copy-start.3
  568.1 0.8 copy-start.4
  568.9 1.8 copy-start.3
  571.5 0.8 copy-start.4
  572.3 1.8 copy-start.3
  574.9 0.8 copy-start.4
  575.7 1.8 copy-start.3
  578.4 0.8 copy-start.4
  579.2 1.8 copy-start.3
  581.8 0.8 copy-start.4
  582.6 1.8 copy-start.3
  585.2 0.8 copy-start.4
  586.0 1.8 copy-start.3
  588.7 0.8 copy-start.4
  589.5 2.3 copy-start.1
Sparse Core Ops, SparseCore 0:
  20.5 49.3 all-gather.6
  94.0 125.0 all-gather.4
  413.1 64.2 all-gather.8
where the time goes:
time: 602 us; the launch traced here: 598 us
  blocking collectives  308 us (51%)
  local copies, waits for them, and re-layouts  98.8 us (16%)
  matrix products  96.4 us (16%)
  waiting for transfers between devices  42.5 us (7%)
  other arithmetic  23.7 us (4%)
  between operations  14 us (2%)
  starting transfers between devices  12.1 us (2%)
    all_gather x1, blocking collectives, on_device(): lax.all_gather(norm_gain, 'wa', axis=0, tiled=True)  212 us
    all_gather x1, blocking collectives, on_device(): live_piece = lax.all_gather(live_flags, 'ctx', axis=0, tiled=True)  96.4 us
    dot_general x32, matrix products, attend(): jnp.einsum('htgk,khd->htgd', weights.astype(jnp.bfloat16), values_part, p...  69.4 us
    all_to_all x1, waiting for transfers between devices, on_device(): lax.all_to_all(keyvalue_weight, 'wa', split_axis=1, concat_axis=0, tiled=...  41.8 us
    dynamic_slice x64, local copies, waits for them, and re-layouts, advance(): rows_now = lax.dynamic_slice_in_dim(kv_rows, offset, width_block, 0)  35.9 us
    unnamed x17, local copies, waits for them, and re-layouts  30 us
    all_to_all x1, local copies, waits for them, and re-layouts, on_device(): lax.all_to_all(w_query, 'wa', split_axis=1, concat_axis=0, tiled=True)  22.6 us
    reduce_sum x32, other arithmetic, attend(): total = total * factor + jnp.sum(weights, axis=-1)  16.2 us
  transfers between devices with their start and end apart: 5, of which 1 were waited for; matrix products, arithmetic and copies ran while one was open for 31% of the time, Pallas kernels for 0%

commit v1 on v0

--- a/solution.py
+++ b/solution.py
@@ -59,7 +59,10 @@
         jnp.bfloat16
     )
     query_cols, keyval_cols = (
-        lax.all_to_all(w_query, "wa", split_axis=1, concat_axis=0, tiled=True),
+        jnp.concatenate(
+            lax.all_to_all(jnp.stack(jnp.split(w_query, lax.axis_size("wa"), axis=1)), "wa", 0, 0),
+            axis=0,
+        ),
         lax.all_to_all(keyvalue_weight, "wa", split_axis=1, concat_axis=0, tiled=True),
     )
     query_sum = jnp.dot(normed, query_cols, preferred_element_type=jnp.float32)

time: 602 us -> 579 us (0.962)
  local copies, waits for them, and re-layouts: 98.8 us -> 61 us
  waiting for transfers between devices: 42.5 us -> 51.5 us
  other arithmetic: 23.7 us -> 30.6 us
    unnamed x17 -> x16, local copies, waits for them, and re-layouts: 30 us -> 7.36 us
    all_to_all x1 -> x0, local copies, waits for them, and re-layouts: 22.6 us -> none  [on_device(): lax.all_to_all(w_query, 'wa', split_axis=1, concat_axis=0, tiled=True)]
    all_to_all x1, waiting for transfers between devices: 41.8 us -> 50.8 us  [on_device(): lax.all_to_all(keyvalue_weight, 'wa', split_axis=1, concat_axis=0, tiled=...]
    another operation x0 -> x1, local copies, waits for them, and re-layouts: none -> 7.46 us  [on_device(): jnp.stack(jnp.split(w_query, lax.axis_size('wa'), axis=1))]
    another operation x0 -> x1, other arithmetic: none -> 6.86 us  [on_device(): jnp.stack(jnp.split(w_query, lax.axis_size('wa'), axis=1))]
  transfers between devices with their start and end apart: 5 -> 5, of which waited for: 1 -> 1; matrix products, arithmetic and copies ran while one was open for 31% -> 28% of each run, Pallas kernels for 0% -> 0%
where the time goes in v1:
time: 579 us; the launch traced here: 576 us
  blocking collectives  308 us (53%)
  matrix products  96.7 us (17%)
  local copies, waits for them, and re-layouts  61 us (11%)
  waiting for transfers between devices  51.5 us (9%)
  other arithmetic  30.6 us (5%)
  between operations  14 us (2%)
  starting transfers between devices  11.9 us (2%)
    all_gather x1, blocking collectives, on_device(): lax.all_gather(norm_gain, 'wa', axis=0, tiled=True)  212 us
    all_gather x1, blocking collectives, on_device(): live_piece = lax.all_gather(live_flags, 'ctx', axis=0, tiled=True)  96.4 us
    dot_general x32, matrix products, attend(): jnp.einsum('htgk,khd->htgd', weights.astype(jnp.bfloat16), values_part, p...  69.7 us
    all_to_all x1, waiting for transfers between devices, on_device(): lax.all_to_all(keyvalue_weight, 'wa', split_axis=1, concat_axis=0, tiled=...  50.8 us
    dynamic_slice x64, local copies, waits for them, and re-layouts, advance(): rows_now = lax.dynamic_slice_in_dim(kv_rows, offset, width_block, 0)  35.9 us
    reduce_sum x32, other arithmetic, attend(): total = total * factor + jnp.sum(weights, axis=-1)  16.2 us
    dot_general x32, matrix products, attend(): jnp.einsum('thgd,khd->htgk', queries_four, keys_part, preferred_element_t...  15.1 us
  transfers between devices with their start and end apart: 5, of which 1 were waited for; matrix products, arithmetic and copies ran while one was open for 28% of the time, Pallas kernels for 0%

profile of v1, /device:TPU:0, one launch (start us, length us, event | category | flops | bytes accessed | tf_op | source)
XLA Modules:
  0.0 576.5 jit_solution(14168079622279709179)
XLA Ops:
  7.3 6.5 %copy.44 = bf16[2048,1024]{0,1:T(8,128)(2,1)} copy(bf16[2048,1024]{1,0:T(8,128)(2,1)} %param.14) | data formatting | bytes 8388608 | tf_op args[3]
  13.7 4.9 all-to-all-start.1
  18.6 7.5 %slice_bitcast_fusion.11 = (bf16[1,2048,1024]{2,1,0:T(8,128)(2,1)S(1)}, bf16[1,2048,1024]{2,1,0:T(8,128)(2,1)S(1)}, bf16[1,2048,1024]{2,1,0:T(8,128)(2,1)S(1)}, bf16[1,2048,1024]{2,1,0:T(8,128)(2,1)S(1)}) fusion(bf16[2048,4096]{1,0:T(8,128)(2,1)} %param.13), kind=kLoop, calls=%fused_computation.63 | loop fusion | bytes 33554432 | tf_op jit(solution)/shard_map/stack | solution.py:63
  26.1 6.9 %pad_maximum_fusion = bf16[4,2048,1024]{2,1,0:T(8,128)(2,1)} fusion(bf16[1,2048,1024]{2,1,0:T(8,128)(2,1)S(1)} %get-tuple-element.396, bf16[1,2048,1024]{2,1,0:T(8,128)(2,1)S(1)} %get-tuple-element.397, bf16[1,2048,1024]{2,1,0:T(8,128)(2,1)S(1)} %get-tuple-element.395, bf16[1,2048,1024]{2,1,0:T(8,128)(2,1)S(1)} %get-tuple-element.394), kind=kLoop, calls=%fused_computation.54 | loop fusion | flops 25165824 | bytes 33554432 | tf_op jit(solution)/shard_map/stack | solution.py:63
  33.0 50.8 %all-to-all-done.1 = bf16[2048,4,256]{0,2,1:T(8,128)(2,1)} async-done(((bf16[2048,4,256]{0,2,1:T(8,128)(2,1)}), bf16[2048,4,256]{0,2,1:T(8,128)(2,1)}, u32[]{:S(2)}, u32[]{:S(2)}) %all-to-all-start.1) | async-done | bytes 4194336 | tf_op jit(solution)/shard_map/all_to_all | solution.py:66
  83.7 7.0 %all-to-all-start = ((bf16[4,2048,1024]{2,1,0:T(8,128)(2,1)}), bf16[4,2048,1024]{2,1,0:T(8,128)(2,1)}, u32[]{:S(2)}, u32[]{:S(2)}) async-start(bf16[4,2048,1024]{2,1,0:T(8,128)(2,1)} %pad_maximum_fusion), calls=%async_computation | async-start | bytes 33554432 | tf_op jit(solution)/shard_map/all_to_all | solution.py:63
  90.8 1.2 gather_fusion
  92.1 212.0 %all_gather.18 = bf16[8192]{0:T(1024)(128)(2,1)S(1)} all-gather(bf16[2048]{0:T(1024)(128)(2,1)S(1)} %copy-done.5), channel_id=1, replica_groups=mesh['ctx'=32,'wa'=4] {'wa'}, dimensions={0}, use_global_device_ids=true | all-gather | bytes 20480 | tf_op jit(solution)/shard_map/all_gather | solution.py:54
  304.8 96.4 %all-gather = bf16[32,1,384]{2,1,0:T(2,128)(2,1)S(1)} all-gather(bf16[1,1,384]{2,1,0:T(2,128)(2,1)S(1)} %reshape.208), channel_id=1, replica_groups=mesh['ctx'=32,'wa'=4] {'ctx'}, dimensions={0}, use_global_device_ids=true | all-gather | bytes 25344 | tf_op jit(solution)/shard_map/all_gather | solution.py:89
  401.4 6.2 %copy.45 = bf16[4,2048,256]{2,1,0:T(8,128)(2,1)} copy(bf16[4,2048,256]{1,2,0:T(8,128)(2,1)} %bitcast.11) | data formatting | bytes 8388608 | tf_op jit(solution)/shard_map/all_to_all | solution.py:66
  407.6 2.2 fusion.32
  409.9 3.6 convolution_convert_fusion
  413.5 8.3 %fusion.36 = bf16[16,8,8,128]{3,1,2,0:T(8,128)(2,1)S(1)} fusion(bf16[8192,1024]{1,0:T(8,128)(2,1)} %bitcast.9, bf16[128,8192]{1,0:T(8,128)(2,1)S(1)} %copy-done.2, f32[8192]{0:T(1024)S(1)} %convert_element_type.42, f32[128]{0:T(128)S(1)} %add_rsqrt_fusion), kind=kOutput, calls=%fused_computation.66 | convolution fusion | flops 2151940096 | bytes 19169792 | tf_op jit(solution)/shard_map/dot_general | solution.py:68
  421.9 118.2 %while.37 = (s32[]{:T(128)}, f32[1,128,8]{1,2,0:T(8,128)S(1)}, f32[1,128,8]{1,2,0:T(8,128)S(1)}, f32[1,128,8,128]{3,1,2,0:T(8,128)}, bf16[12288]{0:T(1024)(128)(...) while((s32[]{:T(128)}, f32[1,128,8]{1,2,0:T(8,128)S(1)}, ...), condition=%wide.region_4.5_spmd.clone, body=%wide.region_1.4_spmd.clone.sunk | while | flops 274079232 | bytes 8982191 | solution.py:47
  422.0 1.0 constant_dynamic-slice_fusion.5
  423.6 1.6 fusion.64
  425.9 1.0 constant_dynamic-slice_fusion.5
  427.5 2.7 fusion.64
  430.9 1.0 constant_dynamic-slice_fusion.5
  432.5 2.7 fusion.64
  435.9 1.0 constant_dynamic-slice_fusion.5
  437.5 2.7 fusion.64
  440.8 1.0 constant_dynamic-slice_fusion.5
  442.4 2.7 fusion.64
  445.8 1.0 constant_dynamic-slice_fusion.5
  447.4 2.7 fusion.64
  450.8 1.0 constant_dynamic-slice_fusion.5
  452.4 2.7 fusion.64
  455.7 1.0 constant_dynamic-slice_fusion.5
  457.3 2.8 fusion.64
  460.8 1.0 constant_dynamic-slice_fusion.5
  462.4 2.7 fusion.64
  465.7 1.0 constant_dynamic-slice_fusion.5
  467.3 2.7 fusion.64
  470.7 1.0 constant_dynamic-slice_fusion.5
  472.3 2.7 fusion.64
  475.7 1.0 constant_dynamic-slice_fusion.5
  477.3 2.7 fusion.64
  480.6 1.0 constant_dynamic-slice_fusion.5
  482.2 2.7 fusion.64
  485.6 1.0 constant_dynamic-slice_fusion.5
  487.2 2.7 fusion.64
  490.6 1.0 constant_dynamic-slice_fusion.5
  492.2 2.7 fusion.64
  497.1 2.7 fusion.64
  500.5 1.0 constant_dynamic-slice_fusion.5
  502.1 2.7 fusion.64
  507.1 2.7 fusion.64
  512.0 2.7 fusion.64
  517.0 2.7 fusion.64
  522.0 2.7 fusion.64
  526.9 2.7 fusion.64
  531.9 2.7 fusion.64
  536.8 2.7 fusion.64
  540.1 27.5 %while.36 = (s32[]{:T(128)}, f32[1,128,8]{1,2,0:T(8,128)S(1)}, f32[1,128,8]{1,2,0:T(8,128)S(1)}, f32[1,128,8,128]{3,1,2,0:T(8,128)}, bf16[4096,256]{1,0:T(8,128)...) while((s32[]{:T(128)}, f32[1,128,8]{1,2,0:T(8,128)S(1)}, ...), condition=%wide.region_8.9_spmd.clone, body=%wide.region_5.8_spmd.clone.sunk | while | flops 274009728 | bytes 13440223 | solution.py:47
  540.2 1.0 constant_dynamic-slice_fusion.4
  543.6 1.0 constant_dynamic-slice_fusion.4
  547.0 1.0 constant_dynamic-slice_fusion.4
  550.5 1.0 constant_dynamic-slice_fusion.4
  553.9 1.0 constant_dynamic-slice_fusion.4
  557.4 1.0 constant_dynamic-slice_fusion.4
  560.8 1.0 constant_dynamic-slice_fusion.4
  564.2 1.0 constant_dynamic-slice_fusion.4
  567.7 1.3 divide_convert_fusion
  (323 shorter events, 58.4 us)
Async XLA Ops:
  6.5 84.2 %copy-start = (bf16[2048,256]{1,0:T(8,128)(2,1)S(1)}, bf16[2048,256]{1,0:T(8,128)(2,1)}, u32[]{:S(2)}) copy-start(bf16[2048,256]{1,0:T(8,128)(2,1)} %param.15) | copy-start | bytes 3145732
  6.5 401.1 %all-gather.7.cloned.1.call-start = ((), (), s32[]{:S(2)}) async-start(), calls=%async_computation.3 | async-start | bytes 2621440 | tf_op jit(solution)/shard_map/all_gather | solution.py:53
  13.7 70.0 %all-to-all-start.1 = ((bf16[2048,4,256]{0,2,1:T(8,128)(2,1)}), bf16[2048,4,256]{0,2,1:T(8,128)(2,1)}, u32[]{:S(2)}, u32[]{:S(2)}) async-start(bf16[2048,4,256]{0,2,1:T(8,128)(2,1)} %bitcast.165), calls=%async_computation.1 | async-start | bytes 8388608 | tf_op jit(solution)/shard_map/all_to_all | solution.py:66
  32.9 57.8 %copy-start.6 = (s32[1,3]{1,0:T(1,128)S(1)}, s32[1,3]{1,0:T(1,128)}, u32[]{:S(2)}) copy-start(s32[1,3]{1,0:T(1,128)} %param.16) | copy-start | bytes 40
  32.9 59.2 %copy-start.5 = (bf16[2048]{0:T(1024)(128)(2,1)S(1)}, bf16[2048]{0:T(1024)(128)(2,1)}, u32[]{:S(2)}) copy-start(bf16[2048]{0:T(1024)(128)(2,1)} %param.12) | copy-start | bytes 12292
  83.7 329.8 %all-to-all-start = ((bf16[4,2048,1024]{2,1,0:T(8,128)(2,1)}), bf16[4,2048,1024]{2,1,0:T(8,128)(2,1)}, u32[]{:S(2)}, u32[]{:S(2)}) async-start(bf16[4,2048,1024]{2,1,0:T(8,128)(2,1)} %pad_maximum_fusion), calls=%async_computation | async-start | bytes 33554432 | tf_op jit(solution)/shard_map/all_to_all | solution.py:63
  90.7 331.2 %all-gather.5.cloned.1.call-start = ((), (), s32[]{:S(2)}) async-start(), calls=%async_computation.2 | async-start | bytes 6488064 | tf_op jit(solution)/shard_map/all_gather | solution.py:88
  92.0 448.1 %all-gather.9.cloned.1.call-start = ((), (), s32[]{:S(2)}) async-start(), calls=%async_computation.4 | async-start | bytes 2162688 | tf_op jit(solution)/shard_map/all_gather | solution.py:102
  407.6 2.2 copy-start.2
  540.1 1.9 copy-start.3
  542.8 0.8 copy-start.4
  543.6 1.8 copy-start.3
  546.2 0.8 copy-start.4
  547.0 1.8 copy-start.3
  549.7 0.8 copy-start.4
  550.5 1.8 copy-start.3
  553.1 0.8 copy-start.4
  553.9 1.8 copy-start.3
  556.5 0.8 copy-start.4
  557.4 1.8 copy-start.3
  560.0 0.8 copy-start.4
  560.8 1.8 copy-start.3
  563.4 0.8 copy-start.4
  564.2 1.8 copy-start.3
  566.9 0.8 copy-start.4
  567.7 2.3 copy-start.1
Sparse Core Ops, SparseCore 0:
  9.0 48.8 all-gather.6
  94.5 125.0 all-gather.4
  413.6 64.2 all-gather.8
